TPU v7x, 32 devices: a whole 2x2x4 slice. The times are simulated.
32 devices in a mesh: stream: 2 (over y), seq: 8 (over z, core), tensor: 2 (over x).
Axes of the slice: x: 2, y: 2, z: 4, core: 2. Of those that a mesh axis runs over, the one named last changes fastest.
Arguments:
- hidden: bfloat16 [2, 1, 4096, 4096], P('stream', None, 'seq', 'tensor'), may hold values from -32 to 32
- norm_gain: float32 [4096], replicated, may hold values from 0.1 to 1.9
- query_weight: bfloat16 [4096, 4096], P('seq', 'tensor'), may hold values from -1 to 1
- key_weight: bfloat16 [4096, 1024], P('seq', 'tensor'), may hold values from -24 to 24
- value_projection_weight: bfloat16 [4096, 1024], P('seq', 'tensor'), may hold values from -0.09375 to 0.09375
- out_weight: bfloat16 [4096, 4096], P('tensor', 'seq'), may hold values from -0.125 to 0.125
Outputs:
- cross_out: bfloat16 [2, 1, 4096, 4096], P('stream', None, 'seq', 'tensor')
All inputs are finite; a program needn't handle non-finite values.
Results may differ from a plain program's by a relative error of at most 0.014.
The roundings to bfloat16 on the way count: a program that leaves them out, or rounds other values in their place, can miss the bound.
Values may be sent and summed in bfloat16 or wider, within the bound.
A program may use at most 256 MiB of HBM per device.

v0:
```python
import functools

import jax
import jax.numpy as jnp
from jax import lax
from jax.experimental import pallas as pl
from jax.experimental.pallas import tpu as pltpu
from jax.sharding import PartitionSpec as P

HEAD_DIM = 128
ROW_CHUNKS = 2
KEY_BLOCK = 1024
LOG2E = 1.4426950408889634


def swap_pairs(block, axis):
    count = lax.axis_size(axis)
    return lax.ppermute(block, axis, [(i, i ^ 1) for i in range(count)])


def attend_kernel(repeat, start_ref, q_ref, k_ref, v_ref, o_ref, m_ref, l_ref, acc_ref):
    step = pl.program_id(1)
    rows = q_ref.shape[0]
    keys = k_ref.shape[0]
    start = start_ref[0]
    last = (start + rows - 1) // keys
    scale = LOG2E * HEAD_DIM ** (-0.5)

    @pl.when(step == 0)
    def _():
        m_ref[...] = jnp.full_like(m_ref, -1e30)
        l_ref[...] = jnp.zeros_like(l_ref)
        acc_ref[...] = jnp.zeros_like(acc_ref)

    def update(masked):
        k = k_ref[...]
        v = v_ref[...]
        if masked:
            frame = start + lax.broadcasted_iota(jnp.int32, (keys, rows), 1)
            key = step * keys + lax.broadcasted_iota(jnp.int32, (keys, rows), 0)
            allowed = key <= frame

        def scored(r):
            q = q_ref[:, r * HEAD_DIM:(r + 1) * HEAD_DIM]
            return lax.dot_general(k, q, (((1,), (1,)), ((), ())), preferred_element_type=jnp.float32)

        following = scored(0)
        for r in range(repeat):
            s = following
            if r + 1 < repeat:
                following = scored(r + 1)
            if masked:
                s = jnp.where(allowed, s, -1e30)
            top = jnp.max(s, axis=0, keepdims=True) * scale
            before = m_ref[r]
            fresh = jnp.maximum(before, top)
            m_ref[r] = fresh
            alpha = jnp.exp2(before - fresh)
            p = jnp.exp2(s * scale - fresh)
            l_ref[r] = alpha * l_ref[r] + jnp.sum(p, axis=0, keepdims=True)
            acc_ref[r] = alpha * acc_ref[r] + lax.dot_general(
                v, p.astype(jnp.bfloat16), (((0,), (0,)), ((), ())), preferred_element_type=jnp.float32
            )

    @pl.when(step < last)
    def _():
        update(False)

    @pl.when(step == last)
    def _():
        update(True)
        for r in range(repeat):
            attended = (acc_ref[r] / l_ref[r]).T
            o_ref[:, r * HEAD_DIM:(r + 1) * HEAD_DIM] = attended.astype(o_ref.dtype)


def attend(start, queries, keys_values, repeat):
    rows, width = queries.shape
    count = keys_values.shape[0]
    groups = width // (repeat * HEAD_DIM)
    block = min(KEY_BLOCK, count)

    def at(step, start_ref):
        return jnp.minimum(step, (start_ref[0] + rows - 1) // block)

    return pl.pallas_call(
        functools.partial(attend_kernel, repeat),
        out_shape=jax.ShapeDtypeStruct((rows, width), jnp.bfloat16),
        grid_spec=pltpu.PrefetchScalarGridSpec(
            num_scalar_prefetch=1,
            grid=(groups, count // block),
            in_specs=[
                pl.BlockSpec((rows, repeat * HEAD_DIM), lambda g, i, s: (0, g)),
                pl.BlockSpec((block, HEAD_DIM), lambda g, i, s: (at(i, s), g)),
                pl.BlockSpec((block, HEAD_DIM), lambda g, i, s: (at(i, s), groups + g)),
            ],
            out_specs=pl.BlockSpec((rows, repeat * HEAD_DIM), lambda g, i, s: (0, g)),
            scratch_shapes=[
                pltpu.VMEM((repeat, 1, rows), jnp.float32),
                pltpu.VMEM((repeat, 1, rows), jnp.float32),
                pltpu.VMEM((repeat, HEAD_DIM, rows), jnp.float32),
            ],
        ),
        compiler_params=pltpu.CompilerParams(
            dimension_semantics=("arbitrary", "arbitrary"), vmem_limit_bytes=32 * 1024 * 1024
        ),
        cost_estimate=pl.CostEstimate(
            flops=8 * rows * count * width,
            bytes_accessed=2 * (2 * rows * width + keys_values.size),
            transcendentals=rows * count * width // HEAD_DIM,
        ),
    )(start.reshape(1), queries, keys_values, keys_values)


SUBS = 4


def line_order(z):
    first = z - 1 + 2 * ((3 - z) // 3)
    third = 3 * (1 - z // 2)
    return (z, first, 6 - z - first - third, third)


def remote(src, dst, send, recv, device):
    return pltpu.make_async_remote_copy(
        src_ref=src, dst_ref=dst, send_sem=send, recv_sem=recv, device_id=device, device_id_type=pl.DeviceIdType.MESH
    )


def greet(z, last, devices, up, down):
    barrier = pltpu.get_barrier_semaphore()

    def hello(device):
        pl.semaphore_signal(barrier, inc=1, device_id=device, device_id_type=pl.DeviceIdType.MESH)

    for device in devices:
        hello(device)

    @pl.when(z < last)
    def _():
        hello(up)

    @pl.when(z > 0)
    def _():
        hello(down)

    inner = jnp.where((z > 0) & (z < last), 1, 0)
    pl.semaphore_wait(barrier, len(devices) + 1 + inner)


def project_kernel(
    gain_ref, hidden_ref, wq_ref, wk_ref, wv_ref, q_ref, kv_ref,
    w, hid, normed, acc,
    local_sem, x_s, x_r, z_s, z_r, y_s, y_r, c_s, c_r, own_s, own_r,
):
    last = 3
    c = lax.axis_index("stream")
    s = lax.axis_index("seq")
    t = lax.axis_index("tensor")
    z, k = s // 2, s % 2
    depth = wq_ref.shape[0]
    half = depth // 2
    rows = half // SUBS
    q_width, kv_width = wq_ref.shape[1], wk_ref.shape[1]
    frames = hid.shape[1]
    step = frames // SUBS
    at = {"stream": c, "seq": s, "tensor": t}
    up, down = {**at, "seq": s + 2}, {**at, "seq": s - 2}
    beside, mate, across = {**at, "stream": 1 - c}, {**at, "seq": 2 * z + 1 - k}, {**at, "tensor": 1 - t}
    greet(z, last, (beside, mate, across), up, down)

    own = pl.multiple_of(s * depth, depth)
    fills = [
        pltpu.make_async_copy(wq_ref, w.at[pl.ds(own, depth), pl.ds(0, q_width)], local_sem.at[0]),
        pltpu.make_async_copy(wk_ref, w.at[pl.ds(own, depth), pl.ds(q_width, kv_width)], local_sem.at[1]),
        pltpu.make_async_copy(wv_ref, w.at[pl.ds(own, depth), pl.ds(q_width + kv_width, kv_width)], local_sem.at[2]),
    ]
    mine = pltpu.make_async_copy(hidden_ref, hid.at[t], local_sem.at[3])
    for copy in fills:
        copy.start()
    mine.start()

    def crossing(piece):
        start = pl.multiple_of(piece * step, step)
        return remote(
            hidden_ref.at[pl.ds(start, step)], hid.at[t, pl.ds(start, step)], x_s.at[piece], x_r.at[piece], across
        )

    for piece in range(SUBS):
        crossing(piece).start()
    for copy in fills:
        copy.wait()

    def part(source, core, side, sub):
        start = pl.multiple_of(source * (2 * depth) + core * depth + side * half + sub * rows, rows)
        return w.at[pl.ds(start, rows)]

    def source(way, hop):
        return z - hop if way == 0 else z + hop

    def along(way, hop, sub):
        view = part(source(way, hop), k, c, sub)
        return remote(view, view, z_s.at[way, hop, sub], z_r.at[way, hop, sub], up if way == 0 else down)

    def sideways(way, hop, sub):
        view = part(source(way, hop), k, c, sub)
        return remote(view, view, y_s.at[way, hop - 1, sub], y_r.at[way, hop - 1, sub], beside)

    def inward(way, kind, hop, sub):
        view = part(source(way, hop), k, c if kind == 0 else 1 - c, sub)
        return remote(view, view, c_s.at[way, kind, hop - 1, sub], c_r.at[way, kind, hop - 1, sub], mate)

    sends = (z < last, z > 0)

    def arrives(way, hop):
        return z >= hop if way == 0 else z + hop <= last

    def each_sub(action):
        @pl.loop(0, SUBS)
        def _(sub):
            action(sub)

    def leave(sub):
        for way in range(2):
            @pl.when(sends[way])
            def _():
                along(way, 0, sub).start()

    each_sub(leave)
    block = w.at[pl.ds(own, depth)]
    share = remote(block, block, own_s, own_r, mate)
    share.start()

    def pass_on(hop, sub):
        for way in range(2):
            @pl.when(arrives(way, hop))
            def _():
                along(way, hop - 1, sub).wait_recv()
                if hop < last:
                    @pl.when(sends[way])
                    def _():
                        along(way, hop, sub).start()
                sideways(way, hop, sub).start()
                inward(way, 0, hop, sub).start()

    def pass_in(hop, sub):
        for way in range(2):
            @pl.when(arrives(way, hop))
            def _():
                sideways(way, hop, sub).wait_recv()
                inward(way, 1, hop, sub).start()

    def gathered(hop):
        def action(sub):
            for way in range(2):
                @pl.when(arrives(way, hop))
                def _():
                    inward(way, 0, hop, sub).wait_recv()
                    inward(way, 1, hop, sub).wait_recv()

        each_sub(action)

    tall = 16

    def norm(sub):
        crossing(sub).wait_recv()

        @pl.loop(0, step // tall)
        def _(i):
            at_rows = pl.ds(pl.multiple_of(sub * step + i * tall, tall), tall)
            low = hid[0, at_rows, :].astype(jnp.float32)
            high = hid[1, at_rows, :].astype(jnp.float32)
            total = jnp.sum(low * low, axis=1, keepdims=True) + jnp.sum(high * high, axis=1, keepdims=True)
            inverse_rms = lax.rsqrt(total / (2 * low.shape[1]) + 1e-05)
            wide = normed.shape[2]
            for group in range(4):
                x = (low if group < 2 else high)[:, (group % 2) * wide:(group % 2 + 1) * wide]
                gain = gain_ref[:, group * wide:(group + 1) * wide]
                normed[group, at_rows, :] = (x * inverse_rms * gain).astype(jnp.bfloat16)

    order = line_order(z)
    tile = min(512, kv_width)

    def dot(place, index):
        group = order[place]
        columns = pl.ds(pl.multiple_of(index * tile, tile), tile)
        return jnp.dot(
            normed[group],
            w[pl.ds(pl.multiple_of(group * 2 * depth, 2 * depth), 2 * depth), columns],
            preferred_element_type=jnp.float32,
        ), columns

    def project(place, low, high):
        @pl.loop(low, high)
        def _(index):
            value, columns = dot(place, index)
            if place == 0:
                acc[:, columns] = value
            else:
                acc[:, columns] += value

    tiles = (q_width + 2 * kv_width) // tile

    each_sub(lambda sub: pass_on(1, sub))
    mine.wait()

    def second(sub):
        pass_on(2, sub)
        pass_in(1, sub)
        norm(sub)

    each_sub(second)
    share.wait_recv()
    gathered(1)
    cut = tiles // 2
    for sub in range(SUBS):
        pass_on(3, sub)
        pass_in(2, sub)
        low = (sub % 2) * cut
        project(sub // 2, low, low + cut if sub % 2 == 0 else tiles)
    each_sub(lambda sub: pass_in(3, sub))
    gathered(2)
    project(2, 0, tiles)
    gathered(3)

    @pl.loop(0, q_width // tile)
    def _(index):
        value, columns = dot(3, index)
        q_ref[:, columns] = (acc[:, columns] + value).astype(jnp.bfloat16)

    for index in range(2 * kv_width // tile):
        value, columns = dot(3, q_width // tile + index)
        kv_ref[:, index * tile:(index + 1) * tile] = (acc[:, columns] + value).astype(jnp.bfloat16)

    share.wait_send()

    def settle(sub):
        crossing(sub).wait_send()
        for way in range(2):
            for hop in range(last):
                @pl.when(sends[way] & (arrives(way, hop) if hop else True))
                def _():
                    along(way, hop, sub).wait_send()
            for hop in range(1, last + 1):
                @pl.when(arrives(way, hop))
                def _():
                    sideways(way, hop, sub).wait_send()
                    inward(way, 0, hop, sub).wait_send()
                    inward(way, 1, hop, sub).wait_send()

    each_sub(settle)


def projected(hidden, norm_gain, query_weight, key_weight, value_weight):
    frames, features = hidden.shape
    depth, q_width = query_weight.shape
    kv_width = key_weight.shape[1]
    total = q_width + 2 * kv_width
    dma = pltpu.SemaphoreType.DMA
    anywhere = pl.BlockSpec(memory_space=pl.ANY)
    vmem = pl.BlockSpec(memory_space=pltpu.VMEM)
    return pl.pallas_call(
        project_kernel,
        out_shape=(
            jax.ShapeDtypeStruct((frames, q_width), jnp.bfloat16),
            jax.ShapeDtypeStruct((frames, 2 * kv_width), jnp.bfloat16),
        ),
        in_specs=[vmem] + [anywhere] * 4,
        out_specs=(vmem, vmem),
        scratch_shapes=[
            pltpu.VMEM((8 * depth, total), jnp.bfloat16),
            pltpu.VMEM((2, frames, features), jnp.bfloat16),
            pltpu.VMEM((4, frames, features // 2), jnp.bfloat16),
            pltpu.VMEM((frames, total), jnp.float32),
            dma((4,)), dma((SUBS,)), dma((SUBS,)),
            dma((2, 3, SUBS)), dma((2, 3, SUBS)),
            dma((2, 3, SUBS)), dma((2, 3, SUBS)),
            dma((2, 2, 3, SUBS)), dma((2, 2, 3, SUBS)),
            dma, dma,
        ],
        compiler_params=pltpu.CompilerParams(
            collective_id=0, has_side_effects=True, vmem_limit_bytes=58 * 1024 * 1024
        ),
        cost_estimate=pl.CostEstimate(
            flops=2 * frames * 8 * depth * total, bytes_accessed=4 * hidden.size, transcendentals=frames
        ),
    )(norm_gain.reshape(1, -1), hidden, query_weight, key_weight, value_weight)


def cross_kernel(
    repeat, q_ref, kv_ref, wo_ref, out_ref,
    kv, wo, m_ref, l_ref, acc_ref, attended, kept, leaving, came,
    local_sem, swap_s, swap_r, k_s, k_r, kc_s, kc_r,
    z_s, z_r, y_s, y_r, c_s, c_r, own_s, own_r, x_s, x_r,
):
    last = 3
    c = lax.axis_index("stream")
    s = lax.axis_index("seq")
    t = lax.axis_index("tensor")
    z, k = s // 2, s % 2
    frames = q_ref.shape[0]
    kv_width = kv_ref.shape[1] // 2
    heads = kv_width // HEAD_DIM
    depth, block = wo_ref.shape
    half = depth // 2
    rows = half // SUBS
    keys = frames // SUBS
    scale = LOG2E * HEAD_DIM ** (-0.5)
    at = {"stream": c, "seq": s, "tensor": t}
    up, down = {**at, "seq": s + 2}, {**at, "seq": s - 2}
    beside, mate, across = {**at, "stream": 1 - c}, {**at, "seq": 2 * z + 1 - k}, {**at, "tensor": 1 - t}
    greet(z, last, (beside, mate, across), up, down)
    sends = (z < last, z > 0)

    def each_sub(action):
        @pl.loop(0, SUBS)
        def _(sub):
            action(sub)

    def key_rows(hop, sub):
        start = pl.multiple_of((2 * (z - hop) + k) * frames + sub * keys, keys)
        return kv.at[pl.ds(start, keys)]

    def swap(sub):
        start = pl.multiple_of(sub * keys, keys)
        return remote(kv_ref.at[pl.ds(start, keys)], key_rows(0, sub), swap_s.at[sub], swap_r.at[sub], beside)

    def climb(hop, sub):
        view = key_rows(hop, sub)
        return remote(view, view, k_s.at[hop, sub], k_r.at[hop, sub], up)

    def hand(hop, sub):
        view = key_rows(hop, sub)
        return remote(view, view, kc_s.at[hop, sub], kc_r.at[hop, sub], mate)

    def source(way, hop):
        return z - hop if way == 0 else z + hop

    def part(origin, core, side, sub):
        start = pl.multiple_of(side * half + sub * rows, rows)
        return wo.at[2 * origin + core, pl.ds(start, rows)]

    def along(way, hop, sub):
        view = part(source(way, hop), k, c, sub)
        return remote(view, view, z_s.at[way, hop, sub], z_r.at[way, hop, sub], up if way == 0 else down)

    def sideways(way, hop, sub):
        view = part(source(way, hop), k, c, sub)
        return remote(view, view, y_s.at[way, hop - 1, sub], y_r.at[way, hop - 1, sub], beside)

    def inward(way, kind, hop, sub):
        view = part(source(way, hop), k, c if kind == 0 else 1 - c, sub)
        return remote(view, view, c_s.at[way, kind, hop - 1, sub], c_r.at[way, kind, hop - 1, sub], mate)

    def arrives(way, hop):
        return z >= hop if way == 0 else z + hop <= last

    def pass_on(way, hop, sub):
        @pl.when(arrives(way, hop))
        def _():
            along(way, hop - 1, sub).wait_recv()
            if hop < last:
                @pl.when(sends[way])
                def _():
                    along(way, hop, sub).start()
            sideways(way, hop, sub).start()
            inward(way, 0, hop, sub).start()

    def pass_in(way, hop, sub):
        @pl.when(arrives(way, hop))
        def _():
            sideways(way, hop, sub).wait_recv()
            inward(way, 1, hop, sub).start()

    def gathered(way, hop):
        @pl.when(arrives(way, hop))
        def _():
            def action(sub):
                inward(way, 0, hop, sub).wait_recv()
                inward(way, 1, hop, sub).wait_recv()

            each_sub(action)

    def pass_keys(hop, sub):
        @pl.when(z >= hop)
        def _():
            climb(hop - 1, sub).wait_recv()
            if hop < last:
                @pl.when(z < last)
                def _():
                    climb(hop, sub).start()
            hand(hop, sub).start()

    def attend_to(head, start, count, masked):
        at_keys = pl.ds(pl.multiple_of(start, count), count)
        keys_here = kv[at_keys, pl.ds(pl.multiple_of(head * HEAD_DIM, HEAD_DIM), HEAD_DIM)]
        values_here = kv[at_keys, pl.ds(pl.multiple_of(kv_width + head * HEAD_DIM, HEAD_DIM), HEAD_DIM)]
        if masked:
            allowed = lax.broadcasted_iota(jnp.int32, (count, frames), 0) <= lax.broadcasted_iota(
                jnp.int32, (count, frames), 1
            )

        def scored(r):
            q = q_ref[:, pl.ds(pl.multiple_of((head * repeat + r) * HEAD_DIM, HEAD_DIM), HEAD_DIM)]
            return lax.dot_general(
                keys_here, q, (((1,), (1,)), ((), ())), preferred_element_type=jnp.float32
            )

        following = scored(0)
        for r in range(repeat):
            index = head * repeat + r
            scores = following
            if r + 1 < repeat:
                following = scored(r + 1)
            if masked:
                scores = jnp.where(allowed, scores, -1e30)
            top = jnp.max(scores, axis=0, keepdims=True) * scale
            before = m_ref[index]
            fresh = jnp.maximum(before, top)
            m_ref[index] = fresh
            alpha = jnp.exp2(before - fresh)
            p = jnp.exp2(scores * scale - fresh)
            l_ref[index] = alpha * l_ref[index] + jnp.sum(p, axis=0, keepdims=True)
            acc_ref[index] = alpha * acc_ref[index] + lax.dot_general(
                values_here, p.astype(jnp.bfloat16), (((0,), (0,)), ((), ())), preferred_element_type=jnp.float32
            )

    def attend_own(head):
        attend_to(head, s * frames, frames, True)

        @pl.when(k == 1)
        def _():
            attend_to(head, (s - 1) * frames, frames, False)

    def attend_hop(hop, head):
        @pl.when(z >= hop)
        def _():
            attend_to(head, (z - hop) * 2 * frames, 2 * frames, False)

    def keys_held(hop):
        @pl.when(z >= hop)
        def _():
            each_sub(lambda sub: hand(hop, sub).wait_recv())

    order = line_order(z)

    def carry(slot):
        return remote(leaving.at[slot], came.at[slot], x_s.at[slot], x_r.at[slot], across)

    def shares(place, core):
        group = order[place]
        share = jnp.dot(attended[...], wo[2 * group + core], preferred_element_type=jnp.float32).astype(jnp.bfloat16)
        slot = (group % 2) * 2 + core

        @pl.when(group // 2 == t)
        def _():
            kept[slot] = share

        @pl.when(group // 2 != t)
        def _():
            leaving[slot] = share
            carry(slot).start()

    each_sub(lambda sub: swap(sub).start())
    fill = pltpu.make_async_copy(wo_ref, wo.at[s], local_sem)
    fill.start()
    fill.wait()

    @pl.when(sends[1])
    def _():
        each_sub(lambda sub: along(1, 0, sub).start())

    whole = remote(wo.at[s], wo.at[s], own_s, own_r, mate)
    whole.start()
    m_ref[...] = jnp.full_like(m_ref, -1e30)
    l_ref[...] = jnp.zeros_like(l_ref)
    acc_ref[...] = jnp.zeros_like(acc_ref)

    def first(sub):
        swap(sub).wait_recv()

        @pl.when(z < last)
        def _():
            climb(0, sub).start()

        hand(0, sub).start()

    each_sub(first)
    keys_held(0)

    for hop in range(1, last + 1):
        def phase(sub):
            pass_keys(hop, sub)
            pass_on(1, hop, sub)
            if hop > 1:
                pass_in(1, hop - 1, sub)
                attend_hop(hop - 1, sub)
            else:
                attend_own(sub)

        each_sub(phase)
        keys_held(hop)
        if hop == last - 1:
            @pl.when(sends[0])
            def _():
                each_sub(lambda sub: along(0, 0, sub).start())

    def fourth(sub):
        pass_on(0, 1, sub)
        pass_in(1, last, sub)
        attend_hop(last, sub)

    each_sub(fourth)

    @pl.loop(0, heads)
    def _(head):
        for r in range(repeat):
            index = head * repeat + r
            out = (acc_ref[index] / l_ref[index]).T.astype(jnp.bfloat16)
            attended[:, pl.ds(pl.multiple_of(index * HEAD_DIM, HEAD_DIM), HEAD_DIM)] = out

    whole.wait_recv()
    for hop in range(1, last + 1):
        gathered(1, hop)
    split = SUBS // 2

    def fifth(sub):
        pass_on(0, 2, sub)
        pass_in(0, 1, sub)

        @pl.when(sub % split == 0)
        def _():
            shares(0, sub // split)

    each_sub(fifth)
    gathered(0, 1)

    def sixth(sub):
        pass_on(0, 3, sub)
        pass_in(0, 2, sub)

        @pl.when(sub % split == 0)
        def _():
            shares(1, sub // split)

    each_sub(sixth)
    gathered(0, 2)
    shares(2, 0)
    shares(2, 1)
    each_sub(lambda sub: pass_in(0, 3, sub))
    gathered(0, 3)
    shares(3, 0)
    shares(3, 1)

    for place in range(4):
        for core in range(2):
            group = order[place]
            slot = (group % 2) * 2 + core

            @pl.when(group // 2 == t)
            def _():
                carry(slot).wait_recv()
                total = kept[slot].astype(jnp.float32) + came[slot].astype(jnp.float32)
                out_ref[:, pl.ds(pl.multiple_of(slot * block, block), block)] = total.astype(jnp.bfloat16)

    whole.wait_send()
    for slot in range(4):
        carry(slot).wait_send()

    def settle(sub):
        swap(sub).wait_send()
        for hop in range(last + 1):
            @pl.when(z >= hop)
            def _():
                hand(hop, sub).wait_send()
                if hop < last:
                    @pl.when(z < last)
                    def _():
                        climb(hop, sub).wait_send()
        for way in range(2):
            for hop in range(last):
                @pl.when(sends[way] & (arrives(way, hop) if hop else True))
                def _():
                    along(way, hop, sub).wait_send()
            for hop in range(1, last + 1):
                @pl.when(arrives(way, hop))
                def _():
                    sideways(way, hop, sub).wait_send()
                    inward(way, 0, hop, sub).wait_send()
                    inward(way, 1, hop, sub).wait_send()

    each_sub(settle)


def crossed(queries, keys_values, out_weight, repeat):
    frames, width = queries.shape
    kv_width = keys_values.shape[1] // 2
    depth, block = out_weight.shape
    count = width // HEAD_DIM
    dma = pltpu.SemaphoreType.DMA
    anywhere = pl.BlockSpec(memory_space=pl.ANY)
    vmem = pl.BlockSpec(memory_space=pltpu.VMEM)
    bf16, f32 = jnp.bfloat16, jnp.float32
    return pl.pallas_call(
        functools.partial(cross_kernel, repeat),
        out_shape=jax.ShapeDtypeStruct((frames, 4 * block), bf16),
        in_specs=[vmem, vmem, anywhere],
        out_specs=vmem,
        scratch_shapes=[
            pltpu.VMEM((8 * frames, 2 * kv_width), bf16),
            pltpu.VMEM((8, depth, block), bf16),
            pltpu.VMEM((count, 1, frames), f32),
            pltpu.VMEM((count, 1, frames), f32),
            pltpu.VMEM((count, HEAD_DIM, frames), f32),
            pltpu.VMEM((frames, width), bf16),
            pltpu.VMEM((4, frames, block), bf16),
            pltpu.VMEM((4, frames, block), bf16),
            pltpu.VMEM((4, frames, block), bf16),
            dma, dma((SUBS,)), dma((SUBS,)),
            dma((3, SUBS)), dma((3, SUBS)),
            dma((4, SUBS)), dma((4, SUBS)),
            dma((2, 3, SUBS)), dma((2, 3, SUBS)),
            dma((2, 3, SUBS)), dma((2, 3, SUBS)),
            dma((2, 2, 3, SUBS)), dma((2, 2, 3, SUBS)),
            dma, dma, dma((4,)), dma((4,)),
        ],
        compiler_params=pltpu.CompilerParams(
            collective_id=1, has_side_effects=True, vmem_limit_bytes=58 * 1024 * 1024
        ),
        cost_estimate=pl.CostEstimate(
            flops=16 * frames * depth * block, bytes_accessed=4 * queries.size, transcendentals=4 * frames * frames * count
        ),
    )(queries, keys_values, out_weight)


def y_share(mine, core, after=None):
    depth = mine.shape[0] // 2
    part = lax.dynamic_slice_in_dim(mine, core * depth, depth, 0)
    near = lax.ppermute(part, "stream", [(0, 1), (1, 0)])
    if after is None:
        return near, swap_pairs(near, "seq")
    near, after = lax.optimization_barrier((near, after))
    return near, swap_pairs(near, "seq"), after


def fits(hidden, query_weight, key_weight):
    meshes = (lax.axis_size("stream"), lax.axis_size("seq"), lax.axis_size("tensor"))
    return (
        meshes == (2, 8, 2)
        and hidden.shape[1:] == (1, 512, 2048)
        and query_weight.shape == (512, 2048)
        and key_weight.shape == (512, 512)
    )


def body(hidden, norm_gain, query_weight, key_weight, value_projection_weight, out_weight):
    if not fits(hidden, query_weight, key_weight):
        return general_body(hidden, norm_gain, query_weight, key_weight, value_projection_weight, out_weight)
    queries, keys_values = projected(
        hidden.reshape(hidden.shape[2:]), norm_gain, query_weight, key_weight, value_projection_weight
    )
    out = crossed(queries, keys_values, out_weight, query_weight.shape[1] // key_weight.shape[1])
    return out.reshape(hidden.shape)


def general_body(hidden, norm_gain, query_weight, key_weight, value_projection_weight, out_weight):
    windows, frame_count = hidden.shape[1], hidden.shape[2]
    n_tensor = lax.axis_size("tensor")
    n_seq = lax.axis_size("seq")
    stream = lax.axis_index("stream")
    tensor = lax.axis_index("tensor")
    seq = lax.axis_index("seq")
    core = seq % 2
    rows = windows * frame_count
    depth = query_weight.shape[0] // 2
    out_half = out_weight.shape[1] // 2

    kv_weight = jnp.concatenate([key_weight, value_projection_weight], axis=1)
    kv_mine = lax.all_gather(
        lax.dynamic_slice_in_dim(kv_weight, stream * depth, depth, 0), "seq", axis=0, tiled=True
    )
    query_mine = lax.all_gather(
        lax.dynamic_slice_in_dim(query_weight, stream * depth, depth, 0), "seq", axis=0, tiled=True
    )
    out_mine = lax.all_gather(
        lax.dynamic_slice_in_dim(out_weight, stream * out_half, out_half, 1), "seq", axis=1, tiled=True
    )

    local = hidden.reshape(rows, hidden.shape[3])
    if n_tensor == 2:
        other = lax.ppermute(local, "tensor", [(0, 1), (1, 0)])
        gathered = jnp.where(
            tensor == 0,
            jnp.concatenate([local, other], axis=1),
            jnp.concatenate([other, local], axis=1),
        )
    else:
        gathered = lax.all_gather(local, "tensor", axis=1, tiled=True)
    flat = gathered.astype(jnp.float32)
    inverse_rms = lax.rsqrt(jnp.mean(flat * flat, axis=1, keepdims=True) + 1e-05)
    normed = (flat * inverse_rms * norm_gain).astype(jnp.bfloat16)
    split = normed.reshape(rows, n_seq, 2, depth)

    def features(half):
        return lax.dynamic_index_in_dim(split, half, 2, keepdims=False).reshape(rows, n_seq * depth)

    normed_mine = features(stream)
    normed_other = features(1 - stream)
    span = n_seq * depth // 2
    normed_near = lax.dynamic_slice_in_dim(normed_other, core * span, span, 1)
    normed_far = lax.dynamic_slice_in_dim(normed_other, (1 - core) * span, span, 1)

    def project(mine, near, far):
        total = jnp.dot(normed_mine, mine, preferred_element_type=jnp.float32)
        total += jnp.dot(normed_near, near, preferred_element_type=jnp.float32)
        total += jnp.dot(normed_far, far, preferred_element_type=jnp.float32)
        return total.astype(jnp.bfloat16)

    keys_values = project(kv_mine, *y_share(kv_mine, core))
    partner = lax.ppermute(keys_values, "stream", [(0, 1), (1, 0)])
    kv_width = key_weight.shape[1]
    parts = 2 if kv_width % (2 * HEAD_DIM) == 0 else 1
    step = kv_width // parts
    pieces = []
    for part in range(parts):
        columns = jnp.concatenate(
            [partner[:, part * step:(part + 1) * step],
             partner[:, kv_width + part * step:kv_width + (part + 1) * step]],
            axis=1,
        )
        pieces.append(
            lax.all_gather(columns.reshape(windows, frame_count, 2 * step), "seq", axis=1, tiled=True)
        )
    queries = project(query_mine, *y_share(query_mine, core)).reshape(windows, frame_count, -1)
    out_near = out_far = None
    width = out_weight.shape[0] // 2

    repeat = query_weight.shape[1] // key_weight.shape[1]
    chunk = frame_count // ROW_CHUNKS

    def scattered(share):
        if n_tensor == 2:
            wide = share.shape[1] // 2
            away = lax.dynamic_slice_in_dim(share, (1 - tensor) * wide, wide, 1)
            kept = lax.dynamic_slice_in_dim(share, tensor * wide, wide, 1)
            came = lax.ppermute(away, "tensor", [(0, 1), (1, 0)])
            return (kept.astype(jnp.float32) + came.astype(jnp.float32)).astype(jnp.bfloat16)
        return lax.psum_scatter(share, "tensor", scatter_dimension=1, tiled=True)

    outs = []
    q_step = step * repeat
    for window in range(windows):
        early = [
            attend(
                seq * frame_count,
                queries[window][:, part * q_step:(part + 1) * q_step],
                pieces[part][window],
                repeat,
            )
            for part in range(parts - 1)
        ]
        for index in range(ROW_CHUNKS):
            low, high = index * chunk, (index + 1) * chunk
            final = attend(
                seq * frame_count + low,
                queries[window][low:high, (parts - 1) * q_step:],
                pieces[-1][window],
                repeat,
            )
            attended = jnp.concatenate([done[low:high] for done in early] + [final], axis=1)
            share_mine = jnp.dot(attended, out_mine, preferred_element_type=jnp.float32)
            if out_near is None:
                out_near, out_far, attended = y_share(out_mine, core, attended)
            attended_near = lax.dynamic_slice_in_dim(attended, core * width, width, 1)
            attended_far = lax.dynamic_slice_in_dim(attended, (1 - core) * width, width, 1)
            share_other = jnp.dot(attended_near, out_near, preferred_element_type=jnp.float32)
            share_other += jnp.dot(attended_far, out_far, preferred_element_type=jnp.float32)
            mine = scattered(share_mine.astype(jnp.bfloat16)).reshape(chunk, -1, out_half)
            other = scattered(share_other.astype(jnp.bfloat16)).reshape(chunk, -1, out_half)
            outs.append(
                jnp.where(
                    stream == 0, jnp.stack([mine, other], axis=2), jnp.stack([other, mine], axis=2)
                ).reshape(chunk, -1)
            )
    return jnp.concatenate(outs, axis=0).reshape(1, windows, frame_count, -1)


def solution(mesh):
    in_specs = (
        P("stream", None, "seq", "tensor"),
        P(),
        P("seq", "tensor"),
        P("seq", "tensor"),
        P("seq", "tensor"),
        P("tensor", "seq"),
    )
    out_specs = P("stream", None, "seq", "tensor")
    return jax.shard_map(body, mesh=mesh, in_specs=in_specs, out_specs=out_specs, check_vma=False)
```

profile of v0, /device:TPU:24, one launch (start us, length us, event | category | flops | bytes accessed | tf_op | source)
XLA Modules:
  0.0 331.1 jit_solution(14814505400795367430)
XLA Ops:
  0.0 128.0 %shard_map.64 = (bf16[512,2048]{1,0:T(8,128)(2,1)}, bf16[512,1024]{1,0:T(8,128)(2,1)}) custom-call(f32[1,4096]{1,0:T(1,128)} %bitcast.5, bf16[512,2048]{1,0:T(8,128)(2,1)} %bitcast.4, bf16[512,2048]{1,0:T(8,128)(2,1)} %wq_ref.1, bf16[512,512]{1,0:T(8,128)(2,1)} %wk_ref.1, bf16[512,512]{1,0:T(8,128)(2,1)} %wv_ref.1), custom_call_target="tpu_custom_call" | custom-call | flops 12884901888 | bytes 4194304 | tf_op jit(solution)/shard_map/pallas_call | solution.py:362
  128.0 199.9 %shard_map.65 = bf16[512,2048]{1,0:T(8,128)(2,1)} custom-call(bf16[512,2048]{1,0:T(8,128)(2,1)} %get-tuple-element.7.q_ref, bf16[512,1024]{1,0:T(8,128)(2,1)} %get-tuple-element.8.kv_ref, bf16[2048,512]{1,0:T(8,128)(2,1)} %wo_ref.1), custom_call_target="tpu_custom_call" | custom-call | flops 8589934592 | bytes 4194304 | tf_op jit(solution)/shard_map/pallas_call | solution.py:704
  327.9 3.2 copy.8
where the time goes:
time: 332 us; the launch traced here: 331 us
  Pallas kernels  328 us (99%)
    pallas_call x1, Pallas kernels, crossed(): pl.pallas_call(functools.partial(cross_kernel, repeat), out_shape=jax.Sha...  200 us
    pallas_call x1, Pallas kernels, projected(): pl.pallas_call(project_kernel, out_shape=(jax.ShapeDtypeStruct((frames, q...  128 us

commit v1 on v0

--- a/solution.py
+++ b/solution.py
@@ -113,6 +113,7 @@
 
 
 SUBS = 4
+WINDOW = 2
 
 
 def line_order(z):
@@ -220,13 +221,24 @@
         def _(sub):
             action(sub)
 
-    def leave(sub):
+    def leave(way, number):
+        if number < last * SUBS:
+            hop, sub = number // SUBS, number % SUBS
+
+            @pl.when(sends[way] & arrives(way, hop))
+            def _():
+                along(way, hop, sub).start()
+
+    def left(way, number):
+        hop, sub = number // SUBS, number % SUBS
+
+        @pl.when(sends[way] & arrives(way, hop))
+        def _():
+            along(way, hop, sub).wait_send()
+
+    for number in range(WINDOW):
         for way in range(2):
-            @pl.when(sends[way])
-            def _():
-                along(way, 0, sub).start()
-
-    each_sub(leave)
+            leave(way, number)
     block = w.at[pl.ds(own, depth)]
     share = remote(block, block, own_s, own_r, mate)
     share.start()
@@ -236,12 +248,12 @@
             @pl.when(arrives(way, hop))
             def _():
                 along(way, hop - 1, sub).wait_recv()
-                if hop < last:
-                    @pl.when(sends[way])
-                    def _():
-                        along(way, hop, sub).start()
                 sideways(way, hop, sub).start()
                 inward(way, 0, hop, sub).start()
+
+            number = (hop - 1) * SUBS + sub
+            left(way, number)
+            leave(way, number + WINDOW)
 
     def pass_in(hop, sub):
         for way in range(2):
@@ -301,7 +313,8 @@
 
     tiles = (q_width + 2 * kv_width) // tile
 
-    each_sub(lambda sub: pass_on(1, sub))
+    for sub in range(SUBS):
+        pass_on(1, sub)
     mine.wait()
 
     def second(sub):
@@ -309,18 +322,23 @@
         pass_in(1, sub)
         norm(sub)
 
-    each_sub(second)
+    for sub in range(SUBS):
+        second(sub)
     share.wait_recv()
     gathered(1)
-    cut = tiles // 2
     for sub in range(SUBS):
         pass_on(3, sub)
         pass_in(2, sub)
-        low = (sub % 2) * cut
-        project(sub // 2, low, low + cut if sub % 2 == 0 else tiles)
-    each_sub(lambda sub: pass_in(3, sub))
+        low, high = sub * 2 * tiles // SUBS, (sub + 1) * 2 * tiles // SUBS
+        for place in range(2):
+            first, end = max(low - place * tiles, 0), min(high - place * tiles, tiles)
+            if first < end:
+                project(place, first, end)
+    for sub in range(SUBS - 1):
+        pass_in(3, sub)
     gathered(2)
     project(2, 0, tiles)
+    pass_in(3, SUBS - 1)
     gathered(3)
 
     @pl.loop(0, q_width // tile)
@@ -337,10 +355,6 @@
     def settle(sub):
         crossing(sub).wait_send()
         for way in range(2):
-            for hop in range(last):
-                @pl.when(sends[way] & (arrives(way, hop) if hop else True))
-                def _():
-                    along(way, hop, sub).wait_send()
             for hop in range(1, last + 1):
                 @pl.when(arrives(way, hop))
                 def _():
@@ -403,7 +417,7 @@
     heads = kv_width // HEAD_DIM
     depth, block = wo_ref.shape
     half = depth // 2
-    rows = half // SUBS
+    wide = block // SUBS
     keys = frames // SUBS
     scale = LOG2E * HEAD_DIM ** (-0.5)
     at = {"stream": c, "seq": s, "tensor": t}
@@ -437,8 +451,7 @@
         return z - hop if way == 0 else z + hop
 
     def part(origin, core, side, sub):
-        start = pl.multiple_of(side * half + sub * rows, rows)
-        return wo.at[2 * origin + core, pl.ds(start, rows)]
+        return wo.at[2 * origin + core, sub, pl.ds(pl.multiple_of(side * half, half), half)]
 
     def along(way, hop, sub):
         view = part(source(way, hop), k, c, sub)
@@ -542,15 +555,13 @@
         def _():
             each_sub(lambda sub: hand(hop, sub).wait_recv())
 
-    order = line_order(z)
-
     def carry(slot):
         return remote(leaving.at[slot], came.at[slot], x_s.at[slot], x_r.at[slot], across)
 
-    def shares(place, core):
-        group = order[place]
-        share = jnp.dot(attended[...], wo[2 * group + core], preferred_element_type=jnp.float32).astype(jnp.bfloat16)
-        slot = (group % 2) * 2 + core
+    def shares(group, sub):
+        weights = jnp.concatenate([wo[2 * group, sub], wo[2 * group + 1, sub]], axis=1)
+        share = jnp.dot(attended[...], weights, preferred_element_type=jnp.float32).astype(jnp.bfloat16)
+        slot = (group % 2) * SUBS + sub
 
         @pl.when(group // 2 == t)
         def _():
@@ -562,9 +573,14 @@
             carry(slot).start()
 
     each_sub(lambda sub: swap(sub).start())
-    fill = pltpu.make_async_copy(wo_ref, wo.at[s], local_sem)
-    fill.start()
-    fill.wait()
+    fills = [
+        pltpu.make_async_copy(wo_ref.at[:, pl.ds(sub * wide, wide)], wo.at[s, sub], local_sem.at[sub])
+        for sub in range(SUBS)
+    ]
+    for fill in fills:
+        fill.start()
+    for fill in fills:
+        fill.wait()
 
     @pl.when(sends[1])
     def _():
@@ -585,7 +601,13 @@
 
         hand(0, sub).start()
 
+    def climb_after(hop):
+        @pl.when(sends[0] & (z == hop))
+        def _():
+            each_sub(lambda sub: along(0, 0, sub).start())
+
     each_sub(first)
+    climb_after(0)
     keys_held(0)
 
     for hop in range(1, last + 1):
@@ -599,14 +621,46 @@
                 attend_own(sub)
 
         each_sub(phase)
+        climb_after(hop)
         keys_held(hop)
-        if hop == last - 1:
-            @pl.when(sends[0])
+
+    def climbed(number):
+        return number // SUBS + 1, number % SUBS
+
+    def arrive(number):
+        hop, sub = climbed(number)
+
+        @pl.when(arrives(0, hop))
+        def _():
+            along(0, hop - 1, sub).wait_recv()
+
+            @pl.when(sends[0] & (hop < last))
             def _():
-                each_sub(lambda sub: along(0, 0, sub).start())
+                along(0, hop, sub).start()
+
+            sideways(0, hop, sub).start()
+            inward(0, 0, hop, sub).start()
+
+    def spread(number):
+        hop, sub = climbed(number)
+        pass_in(0, hop, sub)
+
+    def work(number):
+        hop, sub = climbed(number)
+
+        @pl.when(arrives(0, hop))
+        def _():
+            inward(0, 0, hop, sub).wait_recv()
+            inward(0, 1, hop, sub).wait_recv()
+            shares(z - hop, sub)
 
     def fourth(sub):
-        pass_on(0, 1, sub)
+        arrive(sub)
+
+        @pl.when(sub > 0)
+        def _():
+            spread(sub - 1)
+
         pass_in(1, last, sub)
         attend_hop(last, sub)
 
@@ -620,51 +674,43 @@
             attended[:, pl.ds(pl.multiple_of(index * HEAD_DIM, HEAD_DIM), HEAD_DIM)] = out
 
     whole.wait_recv()
+    each_sub(lambda sub: shares(z, sub))
     for hop in range(1, last + 1):
         gathered(1, hop)
-    split = SUBS // 2
-
-    def fifth(sub):
-        pass_on(0, 2, sub)
-        pass_in(0, 1, sub)
-
-        @pl.when(sub % split == 0)
-        def _():
-            shares(0, sub // split)
-
-    each_sub(fifth)
-    gathered(0, 1)
-
-    def sixth(sub):
-        pass_on(0, 3, sub)
-        pass_in(0, 2, sub)
-
-        @pl.when(sub % split == 0)
-        def _():
-            shares(1, sub // split)
-
-    each_sub(sixth)
-    gathered(0, 2)
-    shares(2, 0)
-    shares(2, 1)
-    each_sub(lambda sub: pass_in(0, 3, sub))
-    gathered(0, 3)
-    shares(3, 0)
-    shares(3, 1)
-
-    for place in range(4):
+
+        @pl.when(arrives(1, hop))
+        def _():
+            each_sub(lambda sub: shares(z + hop, sub))
+
+    each_sub(lambda number: pl.when(number < SUBS - 2)(lambda: work(number)))
+
+    @pl.loop(SUBS, last * SUBS)
+    def _(number):
+        arrive(number)
+        spread(number - 1)
+        work(number - 2)
+
+    spread(last * SUBS - 1)
+    work(last * SUBS - 2)
+    work(last * SUBS - 1)
+
+    high_first = z // 2
+
+    @pl.loop(0, 2 * SUBS)
+    def _(number):
+        side, sub = number // SUBS, number % SUBS
+        side = side + high_first * (1 - 2 * side)
+        slot = side * SUBS + sub
+        carry(slot).wait_recv()
+        total = (kept[slot].astype(jnp.float32) + came[slot].astype(jnp.float32)).astype(jnp.bfloat16)
         for core in range(2):
-            group = order[place]
-            slot = (group % 2) * 2 + core
-
-            @pl.when(group // 2 == t)
-            def _():
-                carry(slot).wait_recv()
-                total = kept[slot].astype(jnp.float32) + came[slot].astype(jnp.float32)
-                out_ref[:, pl.ds(pl.multiple_of(slot * block, block), block)] = total.astype(jnp.bfloat16)
+            start = pl.multiple_of((side * 2 + core) * block + sub * wide, wide)
+            out_ref[:, pl.ds(start, wide)] = total[:, core * wide:(core + 1) * wide]
 
     whole.wait_send()
-    for slot in range(4):
+
+    @pl.loop(0, 2 * SUBS)
+    def _(slot):
         carry(slot).wait_send()
 
     def settle(sub):
@@ -708,21 +754,21 @@
         out_specs=vmem,
         scratch_shapes=[
             pltpu.VMEM((8 * frames, 2 * kv_width), bf16),
-            pltpu.VMEM((8, depth, block), bf16),
+            pltpu.VMEM((8, SUBS, depth, block // SUBS), bf16),
             pltpu.VMEM((count, 1, frames), f32),
             pltpu.VMEM((count, 1, frames), f32),
             pltpu.VMEM((count, HEAD_DIM, frames), f32),
             pltpu.VMEM((frames, width), bf16),
-            pltpu.VMEM((4, frames, block), bf16),
-            pltpu.VMEM((4, frames, block), bf16),
-            pltpu.VMEM((4, frames, block), bf16),
-            dma, dma((SUBS,)), dma((SUBS,)),
+            pltpu.VMEM((2 * SUBS, frames, 2 * block // SUBS), bf16),
+            pltpu.VMEM((2 * SUBS, frames, 2 * block // SUBS), bf16),
+            pltpu.VMEM((2 * SUBS, frames, 2 * block // SUBS), bf16),
+            dma((SUBS,)), dma((SUBS,)), dma((SUBS,)),
             dma((3, SUBS)), dma((3, SUBS)),
             dma((4, SUBS)), dma((4, SUBS)),
             dma((2, 3, SUBS)), dma((2, 3, SUBS)),
             dma((2, 3, SUBS)), dma((2, 3, SUBS)),
             dma((2, 2, 3, SUBS)), dma((2, 2, 3, SUBS)),
-            dma, dma, dma((4,)), dma((4,)),
+            dma, dma, dma((2 * SUBS,)), dma((2 * SUBS,)),
         ],
         compiler_params=pltpu.CompilerParams(
             collective_id=1, has_side_effects=True, vmem_limit_bytes=58 * 1024 * 1024

time: 332 us -> 308 us (0.928)
  Pallas kernels: 328 us -> 304 us
    pallas_call x1, Pallas kernels: 200 us -> 180 us  [crossed(): pl.pallas_call(functools.partial(cross_kernel, repeat), out_shape=jax.Sha...]
    pallas_call x1, Pallas kernels: 128 us -> 124 us  [projected(): pl.pallas_call(project_kernel, out_shape=(jax.ShapeDtypeStruct((frames, q...]
where the time goes in v1:
time: 308 us; the launch traced here: 307 us
  Pallas kernels  304 us (99%)
  local copies, waits for them, and re-layouts  3.16 us (1%)
    pallas_call x1, Pallas kernels, crossed(): pl.pallas_call(functools.partial(cross_kernel, repeat), out_shape=jax.Sha...  180 us
    pallas_call x1, Pallas kernels, projected(): pl.pallas_call(project_kernel, out_shape=(jax.ShapeDtypeStruct((frames, q...  124 us

profile of v1, /device:TPU:24, one launch (start us, length us, event | category | flops | bytes accessed | tf_op | source)
XLA Modules:
  0.0 307.3 jit_solution(7126768944174005244)
XLA Ops:
  0.0 123.6 %shard_map.64 = (bf16[512,2048]{1,0:T(8,128)(2,1)}, bf16[512,1024]{1,0:T(8,128)(2,1)}) custom-call(f32[1,4096]{1,0:T(1,128)} %bitcast.5, bf16[512,2048]{1,0:T(8,128)(2,1)} %bitcast.4, bf16[512,2048]{1,0:T(8,128)(2,1)} %wq_ref.1, bf16[512,512]{1,0:T(8,128)(2,1)} %wk_ref.1, bf16[512,512]{1,0:T(8,128)(2,1)} %wv_ref.1), custom_call_target="tpu_custom_call" | custom-call | flops 12884901888 | bytes 4194304 | tf_op jit(solution)/shard_map/pallas_call | solution.py:376
  123.7 180.4 %shard_map.65 = bf16[512,2048]{1,0:T(8,128)(2,1)} custom-call(bf16[512,2048]{1,0:T(8,128)(2,1)} %get-tuple-element.7.q_ref, bf16[512,1024]{1,0:T(8,128)(2,1)} %get-tuple-element.8.kv_ref, bf16[2048,512]{1,0:T(8,128)(2,1)} %wo_ref.1), custom_call_target="tpu_custom_call" | custom-call | flops 8589934592 | bytes 4194304 | tf_op jit(solution)/shard_map/pallas_call | solution.py:750
  304.1 3.2 %copy.8 = bf16[1,1,512,2048]{3,2,1,0:T(8,128)(2,1)} copy(bf16[1,1,512,2048]{3,2,1,0:T(8,128)(2,1)} %bitcast.3) | data formatting | bytes 4194304
